TPU v7x, 768 devices: a whole 4x8x12 slice. The times are simulated.
768 devices in a mesh: seq: 96 (over x, y_hi, z), fsdp: 8 (over y_lo, core).
Axes of the slice: x: 4, y: 8 (y_hi: 2, y_lo: 4; y = y_hi * 4 + y_lo), z: 12, core: 2. Of those that a mesh axis runs over, the one named last changes fastest.
Arguments:
- inputs: bfloat16 [3, 24576, 8192], P(None, 'seq', 'fsdp'), may hold values from -6 to 6
- grad_out: bfloat16 [24576, 8192], P('seq', 'fsdp'), may hold values from -6 to 6
- filters: bfloat16 [128, 8192], P('fsdp'), may hold values from -0.5 to 0.5
- short_weights: bfloat16 [3, 3, 8192], P(None, None, 'fsdp'), may hold values from -3.5 to 3.5
Outputs:
- grad_inputs: bfloat16 [3, 24576, 8192], P(None, 'seq', 'fsdp')
- grad_filters: float32 [128, 8192], P('fsdp')
- grad_short: float32 [3, 3, 8192], P(None, None, 'fsdp')
All inputs are finite; a program needn't handle non-finite values.
Results may differ from a plain program's by a relative error of at most 0.0057.
Values may be sent and summed in bfloat16 or wider, within the bound.
A program may use at most 32 MiB of HBM per device.

v0:
```python
import jax
import jax.numpy as jnp
from jax import lax
from jax.sharding import PartitionSpec as P

FILTER_LEN = 128
SHORT_LEN = 3


def from_behind(block, axis, distance):
    devices = range(lax.axis_size(axis))
    route = [(i - distance, i) for i in devices if i - distance in devices]
    return lax.ppermute(block, axis, route)


def packed_total(arrays, axis):
    ends = [0]
    for a in arrays:
        ends.append(ends[-1] + a.size)
    so_far = lax.psum(jnp.concatenate([a.ravel() for a in arrays]), axis)
    return tuple((so_far[b:e].reshape(a.shape) for a, b, e in zip(arrays, ends, ends[1:])))


def depthwise(signal, kernel):
    result = lax.conv_general_dilated(
        signal[None],
        kernel[:, None, :],
        (1,),
        "VALID",
        dimension_numbers=("NWC", "WIO", "NWC"),
        feature_group_count=signal.shape[1],
        preferred_element_type=jnp.float32,
    )
    return result[0]


def short_forward(padded, weights, count):
    lag = weights.shape[1] - 1
    result = weights[:, 0][:, None, :] * padded[:, lag : lag + count]
    for offset in range(1, weights.shape[1]):
        result = (
            result + weights[:, offset][:, None, :] * padded[:, lag - offset : lag - offset + count]
        )
    return result


def short_backward(trailing, weights, count):
    result = weights[:, 0][:, None, :] * trailing[:, 0:count]
    for offset in range(1, weights.shape[1]):
        result = result + weights[:, offset][:, None, :] * trailing[:, offset : offset + count]
    return result


def upper_rows(piece):
    return from_behind(piece, "seq", -1)


def local(inputs, grad_out, filters, short_weights):
    rows = inputs.shape[1]
    lag = SHORT_LEN - 1
    reach = FILTER_LEN - 1
    taps = lax.all_to_all(filters, "fsdp", split_axis=1, concat_axis=0, tiled=True)
    weights = short_weights.astype(jnp.float32)
    span = reach + lag
    outgoing = jnp.concatenate(
        [inputs[0, rows - lag :], inputs[1, rows - span :], inputs[2, rows - span :]], axis=0
    )
    incoming = from_behind(outgoing, "seq", 1)
    prior_q = incoming[:lag]
    prior_k = incoming[lag : lag + span]
    prior_v = incoming[lag + span :]
    earlier = jnp.stack([prior_q, prior_k[span - lag :], prior_v[span - lag :]])
    padded = jnp.concatenate([earlier, inputs], axis=1).astype(jnp.float32)
    shorts = short_forward(padded, weights, rows)
    mixed = (shorts[1] * shorts[2]).astype(jnp.bfloat16)
    prior_shorts = short_forward(
        jnp.stack([prior_k, prior_v]).astype(jnp.float32), weights[1:], reach
    )
    mixed_below = (prior_shorts[0] * prior_shorts[1]).astype(jnp.bfloat16)
    mixed_ext = jnp.concatenate([mixed_below, mixed], axis=0)
    long_out = depthwise(mixed_ext, taps[::-1])
    upstream = grad_out.astype(jnp.float32)
    grad_q = (upstream * long_out).astype(jnp.bfloat16)
    grad_long = (upstream * shorts[0]).astype(jnp.bfloat16)
    following = upper_rows(grad_long[:reach])
    grad_mixed = depthwise(jnp.concatenate([grad_long, following], axis=0), taps)
    grad_k = (grad_mixed * shorts[2]).astype(jnp.bfloat16)
    grad_v = (grad_mixed * shorts[1]).astype(jnp.bfloat16)
    stacked = jnp.stack([grad_q, grad_k, grad_v])
    upper = upper_rows(stacked[:, :lag])
    trailing = jnp.concatenate([stacked, upper], axis=1).astype(jnp.float32)
    grad_inputs = short_backward(trailing, weights, rows).astype(jnp.bfloat16)
    stacked_wide = stacked.astype(jnp.float32)
    short_terms = jnp.stack(
        [
            jnp.sum(stacked_wide * padded[:, lag - offset : lag - offset + rows], axis=1)
            for offset in range(SHORT_LEN)
        ],
        axis=1,
    )
    filter_terms = depthwise(mixed_ext, grad_long)[::-1]
    summed_filter, grad_short = packed_total((filter_terms, short_terms), "seq")
    grad_filters = lax.all_to_all(summed_filter, "fsdp", split_axis=0, concat_axis=1, tiled=True)
    return (grad_inputs, grad_filters, grad_short)


def solution(mesh):
    placed = (P(None, "seq", "fsdp"), P("seq", "fsdp"), P("fsdp", None), P(None, None, "fsdp"))
    return jax.shard_map(
        local,
        mesh=mesh,
        in_specs=placed,
        out_specs=(P(None, "seq", "fsdp"), P("fsdp", None), P(None, None, "fsdp")),
        check_vma=False,
    )
```

profile of v0, /device:TPU:1, one launch (start us, length us, event | category | flops | bytes accessed | tf_op | source)
XLA Modules:
  0.0 1357.2 jit_solution(5432690691682109678)
XLA Ops:
  7.2 0.0 copy-start
  7.2 0.0 copy-start.2
  7.2 1.8 copy.88
  9.0 13.8 %all-to-all-start = ((bf16[16,8,1024]{2,0,1:T(8,128)(2,1)}), bf16[16,8,1024]{2,0,1:T(8,128)(2,1)S(1)}, u32[]{:S(2)}, u32[]{:S(2)}) async-start(bf16[16,8,1024]{2,0,1:T(8,128)(2,1)} %bitcast.64), calls=%async_computation | async-start | bytes 524288 | tf_op jit(solution)/shard_map/all_to_all | solution.py:62
  22.8 0.0 all-reduce.2.cloned.1.call-start
  22.8 0.7 slice_bitcast_fusion.8
  23.5 1.2 slice_bitcast_fusion.4
  24.7 0.1 pad_maximum_fusion.2
  24.9 1.3 collective-permute-start
  26.2 0.0 copy-done.2
  26.3 5.2 all-to-all-done
  31.5 0.3 rev.6
  31.9 6.0 collective-permute-done
  37.9 0.0 copy-done
  37.9 0.5 maximum_convert_fusion
  38.4 0.0 copy-start.1
  38.4 0.9 multiply_add_fusion
  39.3 0.1 copy-done.1
  39.4 0.1 fusion.13
  39.6 1.3 collective-permute-start.1
  40.9 0.1 slice_bitcast_fusion.2
  41.1 0.1 maximum_convert_fusion.2
  41.2 0.3 fusion.14
  41.5 0.1 fusion.22
  41.5 8.2 collective-permute-done.1
  49.7 0.1 maximum_bitcast_fusion.1
  49.8 14.2 %fusion.6 = f32[1,256,1024]{2,0,1:T(1,128)S(1)} fusion(bf16[1,383,1024]{2,1,0:T(8,128)(2,1)S(1)} %maximum_bitcast_fusion.1, bf16[128,1,1024]{2,0,1:T(8,128)(2,1)S(1)} %bitcast.73), kind=kOutput, calls=%fused_computation.16 | convolution fusion | flops 67108864 | bytes 2095104 | tf_op jit(solution)/shard_map/conv_general_dilated | solution.py:25
  63.9 0.5 multiply_convert_fusion.1
  64.5 0.1 maximum_bitcast_fusion
  64.6 13.9 %fusion.8 = f32[1,128,1024]{2,0,1:T(1,128)S(1)} fusion(bf16[1,383,1024]{2,1,0:T(8,128)(2,1)S(1)} %maximum_bitcast_fusion, bf16[256,1,1024]{2,0,1:T(8,128)(2,1)S(1)} %bitcast.67), kind=kOutput, calls=%fused_computation.20 | convolution fusion | flops 67108864 | bytes 1832960 | tf_op jit(solution)/shard_map/conv_general_dilated | solution.py:25
  78.5 14.2 %fusion.10 = f32[1,256,1024]{2,0,1:T(1,128)S(1)} fusion(bf16[1,383,1024]{2,1,0:T(8,128)(2,1)S(1)} %maximum_bitcast_fusion, bf16[128,1,1024]{2,0,1:T(8,128)(2,1)S(1)} %bitcast.76), kind=kOutput, calls=%fused_computation.22 | convolution fusion | flops 67108864 | bytes 2095104 | tf_op jit(solution)/shard_map/conv_general_dilated | solution.py:25
  92.7 0.3 fusion.18
  93.0 1.2 fusion
  94.3 0.1 copy.87
  94.4 0.2 rev.7
  94.7 0.1 copy.61
  94.9 0.8 pad_maximum_fusion.1
  95.7 0.0 all-reduce.2.cloned.1.call-update
  95.7 1179.8 %all-reduce.2.cloned.1.call-done = f32[140288]{0:T(1024)} async-done(((f32[140288]{0:T(1024)}), f32[140288]{0:T(1024)}) %all-reduce.2.cloned.1.call-update) | async-done | bytes 561168 | tf_op jit(solution)/shard_map/psum | solution.py:20
  1275.6 1.1 slice.171
  1276.7 0.9 all_to_all.32
  1277.5 57.5 %all-to-all-start.1 = ((f32[8,16,1024]{2,1,0:T(8,128)}), f32[8,16,1024]{2,1,0:T(8,128)S(1)}, u32[]{:S(2)}, u32[]{:S(2)}) async-start(f32[8,16,1024]{2,1,0:T(8,128)} %all_to_all.32), calls=%async_computation.1 | async-start | bytes 1048576 | tf_op jit(solution)/shard_map/all_to_all | solution.py:103
  1335.0 0.2 pad_maximum_fusion
  1335.2 1.3 collective-permute-start.2
  1336.5 3.5 collective-permute-done.2
  1340.0 0.4 maximum_convert_fusion.1
  1340.4 0.0 slice-start
  1340.4 2.1 fusion.4
  1342.5 0.0 slice-done
  1342.5 0.6 reshape.32
  1343.2 6.4 all-to-all-done.1
  1349.5 0.8 copy.60
  (14 shorter events, 0.2 us)
Async XLA Ops:
  7.2 30.8 %copy-start = (bf16[3,256,1024]{2,1,0:T(8,128)(2,1)S(1)}, bf16[3,256,1024]{2,1,0:T(8,128)(2,1)}, u32[]{:S(2)}) copy-start(bf16[3,256,1024]{2,1,0:T(8,128)(2,1)} %param.4) | copy-start | bytes 4718596
  7.2 19.0 %copy-start.2 = (bf16[3,3,1024]{2,1,0:T(4,128)(2,1)S(1)}, bf16[3,3,1024]{2,1,0:T(4,128)(2,1)}, u32[]{:S(2)}) copy-start(bf16[3,3,1024]{2,1,0:T(4,128)(2,1)} %param.7) | copy-start | bytes 55300
  9.0 22.6 %all-to-all-start = ((bf16[16,8,1024]{2,0,1:T(8,128)(2,1)}), bf16[16,8,1024]{2,0,1:T(8,128)(2,1)S(1)}, u32[]{:S(2)}, u32[]{:S(2)}) async-start(bf16[16,8,1024]{2,0,1:T(8,128)(2,1)} %bitcast.64), calls=%async_computation | async-start | bytes 524288 | tf_op jit(solution)/shard_map/all_to_all | solution.py:62
  22.8 1252.8 %all-reduce.2.cloned.1.call-start = ((), (), s32[]{:S(2)}) async-start(), calls=%async_computation.2 | async-start | bytes 1122304 | tf_op jit(solution)/shard_map/psum | solution.py:20
  24.9 13.0 collective-permute-start
  38.4 1.0 copy-start.1
  39.6 10.1 collective-permute-start.1
  1277.5 72.0 %all-to-all-start.1 = ((f32[8,16,1024]{2,1,0:T(8,128)}), f32[8,16,1024]{2,1,0:T(8,128)S(1)}, u32[]{:S(2)}, u32[]{:S(2)}) async-start(f32[8,16,1024]{2,1,0:T(8,128)} %all_to_all.32), calls=%async_computation.1 | async-start | bytes 1048576 | tf_op jit(solution)/shard_map/all_to_all | solution.py:103
  1335.2 4.8 collective-permute-start.2
  1340.4 2.2 slice-start
Sparse Core Ops, SparseCore 0:
  95.9 1179.6 all-reduce.1
where the time goes:
time: 1360 us
  waiting for transfers between devices  1210 us (89%)
  starting transfers between devices  75.2 us (6%)
  matrix products  42.2 us (3%)
  between operations  14.4 us (1%)
    psum x1, waiting for transfers between devices, packed_total(): so_far = lax.psum(jnp.concatenate([a.ravel() for a in arrays]), axis)  1180 us
    all_to_all x1, starting transfers between devices, local(): lax.all_to_all(summed_filter, 'fsdp', split_axis=0, concat_axis=1, tiled=...  57.5 us
    conv_general_dilated x3, matrix products, depthwise(): lax.conv_general_dilated(signal[None], kernel[:, None, :], (1,), 'VALID',...  42.2 us
  transfers between devices with their start and end apart: 6, of which 6 were waited for; matrix products, arithmetic and copies ran while one was open for 0% of the time, Pallas kernels for 0%

commit v1 on v0

--- a/solution.py
+++ b/solution.py
@@ -1,10 +1,18 @@
+import functools
+
 import jax
 import jax.numpy as jnp
 from jax import lax
+from jax.experimental import pallas as pl
+from jax.experimental.pallas import tpu as pltpu
 from jax.sharding import PartitionSpec as P
 
 FILTER_LEN = 128
 SHORT_LEN = 3
+NX, NYH, NZ = 4, 2, 12
+GROUP = 16
+LINK = jnp.float32
+MESH = pl.DeviceIdType.MESH
 
 
 def from_behind(block, axis, distance):
@@ -13,12 +21,197 @@
     return lax.ppermute(block, axis, route)
 
 
-def packed_total(arrays, axis):
-    ends = [0]
-    for a in arrays:
-        ends.append(ends[-1] + a.size)
-    so_far = lax.psum(jnp.concatenate([a.ravel() for a in arrays]), axis)
-    return tuple((so_far[b:e].reshape(a.shape) for a, b, e in zip(arrays, ends, ends[1:])))
+def reduce_kernel(nf, part, filt_out, short_out, xs, xr, zs, zr, ys, yr, gs, ag, sx, rx, sz, rz, sy, ry, sg, rg, sh, rh, sa, ra):
+    seq = lax.axis_index("seq")
+    fs = lax.axis_index("fsdp")
+    z = lax.rem(seq, NZ)
+    yh = lax.rem(seq // NZ, NYH)
+    x = seq // (NZ * NYH)
+    groups = nf + 1
+    cw = xs.shape[2]
+    owner = z < groups
+
+    def at(ax, ay, az):
+        return (ax * NYH + ay) * NZ + az
+
+    def around_x(d):
+        return at(lax.rem(x + d, NX), yh, z)
+
+    def around_z(d):
+        return at(x, yh, lax.rem(z + d, NZ))
+
+    across = at(x, 1 - yh, z)
+
+    barrier = pltpu.get_barrier_semaphore()
+
+    def greet(s, f):
+        pl.semaphore_signal(barrier, inc=1, device_id=(s, f), device_id_type=MESH)
+
+    for d in range(1, NX):
+        greet(around_x(d), fs)
+    for d in range(1, NZ):
+        greet(around_z(d), fs)
+    greet(across, fs)
+    for f in range(nf):
+        @pl.when(jnp.logical_or(z != fs, fs != f))
+        def _(f=f):
+            greet(at(x, yh, fs), f)
+
+    for c in range(NX):
+        xs[c] = part[:, c * cw:(c + 1) * cw].astype(xs.dtype)
+
+    hearers = jnp.where(z < nf, jnp.where(z == fs, NZ - 1, NZ), 0)
+    pl.semaphore_wait(barrier, NX - 1 + NZ - 1 + 1 + hearers)
+
+    def remote(src, dst, ssem, rsem, s, f):
+        return pltpu.make_async_remote_copy(
+            src_ref=src, dst_ref=dst, send_sem=ssem, recv_sem=rsem, device_id=(s, f), device_id_type=MESH
+        )
+
+    def x_copy(d):
+        return remote(xs.at[lax.rem(x + d, NX)], xr.at[d - 1], sx.at[d - 1], rx.at[d - 1], around_x(d), fs)
+
+    for d in range(1, NX):
+        x_copy(d).start()
+    total = part[:, pl.ds(pl.multiple_of(x * cw, cw), cw)]
+    for d in range(1, NX):
+        x_copy(d).wait_recv()
+        total = total + xr[d - 1].astype(jnp.float32)
+    for g in range(groups):
+        zs[g] = total[g * GROUP:(g + 1) * GROUP]
+
+    def z_copy(d):
+        return remote(zs.at[lax.rem(z + d, NZ)], zr.at[d - 1], sz.at[d - 1], rz.at[d - 1], around_z(d), fs)
+
+    for d in range(1, NZ):
+        @pl.when(lax.rem(z + d, NZ) < groups)
+        def _(d=d):
+            z_copy(d).start()
+
+    def y_copy():
+        return remote(ys, yr, sy, ry, across, fs)
+
+    def g_copy(d, f):
+        return remote(gs, ag.at[x, fs], sg.at[d], rg.at[fs], around_z(d), f)
+
+    def g_landing(f):
+        return remote(ag.at[x, f], ag.at[x, f], sg.at[0], rg.at[f], across, fs)
+
+    def h_copy(d):
+        return remote(ag.at[x, nf], ag.at[x, nf], sh.at[d - 1], rh, around_z(d), fs)
+
+    @pl.when(owner)
+    def _():
+        total = zs[z]
+        for d in range(1, NZ):
+            z_copy(d).wait_recv()
+            total = total + zr[d - 1].astype(jnp.float32)
+        ys[...] = total.astype(ys.dtype)
+        y_copy().start()
+        y_copy().wait_recv()
+        piece = (total + yr[...].astype(jnp.float32)).astype(ag.dtype)
+        y_copy().wait_send()
+
+        @pl.when(z < nf)
+        def _():
+            gs[...] = piece
+
+            @pl.when(z == fs)
+            def _():
+                ag[x, fs] = piece
+
+            for d in range(NZ):
+                @pl.when(jnp.logical_or(d != 0, z != fs))
+                def _(d=d):
+                    g_copy(d, z).start()
+
+        @pl.when(z == nf)
+        def _():
+            ag[x, nf] = piece
+            for d in range(1, NZ):
+                h_copy(d).start()
+
+    for f in range(nf):
+        @pl.when(jnp.logical_or(z != fs, fs != f))
+        def _(f=f):
+            g_landing(f).wait_recv()
+
+    @pl.when(z != nf)
+    def _():
+        h_copy(1).wait_recv()
+
+    def a_copy(d):
+        return remote(ag.at[x], ag.at[x], sa.at[d - 1], ra.at[d - 1], around_x(d), fs)
+
+    def a_landing(d):
+        back = lax.rem(x + NX - d, NX)
+        return remote(ag.at[back], ag.at[back], sa.at[d - 1], ra.at[d - 1], around_x(d), fs)
+
+    for d in range(1, NX):
+        x_copy(d).wait_send()
+    for d in range(1, NX):
+        a_copy(d).start()
+    for d in range(1, NX):
+        a_landing(d).wait_recv()
+    for c in range(NX):
+        for f in range(nf):
+            lo = f * NX * cw + c * cw
+            filt_out[:, lo:lo + cw] = ag[c, f].astype(jnp.float32)
+        short_out[:, c * cw:(c + 1) * cw] = ag[c, nf].astype(jnp.float32)
+
+    for d in range(1, NX):
+        a_copy(d).wait_send()
+    for d in range(1, NZ):
+        @pl.when(lax.rem(z + d, NZ) < groups)
+        def _(d=d):
+            z_copy(d).wait_send()
+
+    @pl.when(z < nf)
+    def _():
+        for d in range(NZ):
+            @pl.when(jnp.logical_or(d != 0, z != fs))
+            def _(d=d):
+                g_copy(d, z).wait_send()
+
+    @pl.when(z == nf)
+    def _():
+        for d in range(1, NZ):
+            h_copy(d).wait_send()
+
+
+def reduced(part, nf):
+    rows, width = part.shape
+    cw = width // NX
+    dma = pltpu.SemaphoreType.DMA
+    vm = pl.BlockSpec(memory_space=pltpu.VMEM)
+    return pl.pallas_call(
+        functools.partial(reduce_kernel, nf),
+        out_shape=(
+            jax.ShapeDtypeStruct((GROUP, nf * width), jnp.float32),
+            jax.ShapeDtypeStruct((GROUP, width), jnp.float32),
+        ),
+        in_specs=[vm],
+        out_specs=(vm, vm),
+        scratch_shapes=[
+            pltpu.VMEM((NX, rows, cw), LINK),
+            pltpu.VMEM((NX - 1, rows, cw), LINK),
+            pltpu.VMEM((NZ, GROUP, cw), LINK),
+            pltpu.VMEM((NZ - 1, GROUP, cw), LINK),
+            pltpu.VMEM((GROUP, cw), LINK),
+            pltpu.VMEM((GROUP, cw), LINK),
+            pltpu.VMEM((GROUP, cw), LINK),
+            pltpu.VMEM((NX, nf + 1, GROUP, cw), LINK),
+            dma((NX - 1,)), dma((NX - 1,)),
+            dma((NZ - 1,)), dma((NZ - 1,)),
+            dma, dma,
+            dma((NZ,)), dma((nf,)),
+            dma((NZ - 1,)), dma,
+            dma((NX - 1,)), dma((NX - 1,)),
+        ],
+        compiler_params=pltpu.CompilerParams(
+            collective_id=0, has_side_effects=True, vmem_limit_bytes=40 * 1024 * 1024
+        ),
+    )(part)
 
 
 def depthwise(signal, kernel):
@@ -57,6 +250,7 @@
 
 def local(inputs, grad_out, filters, short_weights):
     rows = inputs.shape[1]
+    nf = lax.axis_size("fsdp")
     lag = SHORT_LEN - 1
     reach = FILTER_LEN - 1
     taps = lax.all_to_all(filters, "fsdp", split_axis=1, concat_axis=0, tiled=True)
@@ -99,8 +293,11 @@
         axis=1,
     )
     filter_terms = depthwise(mixed_ext, grad_long)[::-1]
-    summed_filter, grad_short = packed_total((filter_terms, short_terms), "seq")
-    grad_filters = lax.all_to_all(summed_filter, "fsdp", split_axis=0, concat_axis=1, tiled=True)
+    width = inputs.shape[2]
+    spare = jnp.zeros((GROUP - 9, width), jnp.float32)
+    part = jnp.concatenate([filter_terms, short_terms.reshape(9, width), spare], axis=0)
+    grad_filters, short_rows = reduced(part, nf)
+    grad_short = short_rows[:9].reshape(3, SHORT_LEN, width)
     return (grad_inputs, grad_filters, grad_short)
 
 

time: 1360 us -> 173 us (0.13)
  the two profiles are of different devices: /device:TPU:1 before, /device:TPU:56 now
where the time goes in v1:
time: 173 us; the launch traced here: 172 us
  Pallas kernels  48.5 us (28%)
  matrix products  42.2 us (24%)
  waiting for transfers between devices  41.8 us (24%)
  starting transfers between devices  23.4 us (14%)
  other arithmetic  8.43 us (5%)
  local copies, waits for them, and re-layouts  7.09 us (4%)
    pallas_call x1, Pallas kernels, reduced(): pl.pallas_call(functools.partial(reduce_kernel, nf), out_shape=(jax.Shape...  48.5 us
    conv_general_dilated x3, matrix products, depthwise(): lax.conv_general_dilated(signal[None], kernel[:, None, :], (1,), 'VALID',...  42.2 us
    ppermute x3, waiting for transfers between devices, from_behind(): return lax.ppermute(block, axis, route)  41.2 us
    ppermute x3, starting transfers between devices, from_behind(): return lax.ppermute(block, axis, route)  17.1 us
    all_to_all x1, starting transfers between devices, local(): lax.all_to_all(filters, 'fsdp', split_axis=1, concat_axis=0, tiled=True)  6.27 us
  transfers between devices with their start and end apart: 4, of which 3 were waited for; matrix products, arithmetic and copies ran while one was open for 2% of the time, Pallas kernels for 28%

profile of v1, /device:TPU:56, one launch (start us, length us, event | category | flops | bytes accessed | tf_op | source)
XLA Modules:
  0.0 172.4 jit_solution(3270333295562028914)
XLA Ops:
  0.6 0.0 copy-start
  0.6 0.0 copy-start.2
  0.7 1.8 %copy.83 = bf16[2,8,8,1024]{3,2,0,1:T(8,128)(2,1)} copy(bf16[2,8,8,1024]{3,2,1,0:T(8,128)(2,1)} %bitcast.68) | data formatting | bytes 524288 | tf_op jit(solution)/shard_map/all_to_all | solution.py:256
  2.4 6.3 %all-to-all-start = ((bf16[16,8,1024]{2,0,1:T(8,128)(2,1)}), bf16[16,8,1024]{2,0,1:T(8,128)(2,1)S(1)}, u32[]{:S(2)}, u32[]{:S(2)}) async-start(bf16[16,8,1024]{2,0,1:T(8,128)(2,1)} %bitcast.59), calls=%async_computation | async-start | bytes 524288 | tf_op jit(solution)/shard_map/all_to_all | solution.py:256
  8.7 0.7 slice_bitcast_fusion.8
  9.4 1.2 slice_bitcast_fusion.4
  10.6 0.1 pad_maximum_fusion.1
  10.8 4.3 %collective-permute-start = (bf16[260,1024]{1,0:T(8,128)(2,1)S(1)}, bf16[260,1024]{1,0:T(8,128)(2,1)S(1)}, u32[]{:S(2)}, u32[]{:S(2)}) collective-permute-start(bf16[260,1024]{1,0:T(8,128)(2,1)S(1)} %pad_maximum_fusion.1), channel_id=1, source_target_pairs={{0,8},{8,16},{16,24},{24,32},{32,40},{40,48},{48,56},{56,64},{64,7... | collective-permute-start | bytes 1597448 | tf_op jit(solution)/shard_map/ppermute | solution.py:21
  15.1 0.0 copy-done.2
  15.2 0.1 pad.2.clone
  15.3 0.6 all-to-all-done
  15.9 0.3 rev.6
  16.2 34.9 %collective-permute-done = bf16[260,1024]{1,0:T(8,128)(2,1)S(1)} collective-permute-done((bf16[260,1024]{1,0:T(8,128)(2,1)S(1)}, bf16[260,1024]{1,0:T(8,128)(2,1)S(1)}, u32[]{:S(2)}, u32[]{:S(2)}) %collective-permute-start) | collective-permute-done | bytes 532512 | tf_op jit(solution)/shard_map/ppermute | solution.py:21
  51.1 0.0 copy-done
  51.1 0.5 maximum_convert_fusion
  51.6 0.0 copy-start.1
  51.6 0.9 multiply_add_fusion
  52.5 0.1 copy-done.1
  52.6 0.1 fusion.13
  52.8 1.9 %collective-permute-start.1 = (bf16[127,1024]{1,0:T(8,128)(2,1)S(1)}, bf16[127,1024]{1,0:T(8,128)(2,1)S(1)}, u32[]{:S(2)}, u32[]{:S(2)}) collective-permute-start(bf16[127,1024]{1,0:T(8,128)(2,1)S(1)} %slice.160), channel_id=1, source_target_pairs={{8,0},{16,8},{24,16},{32,24},{40,32},{48,40},{56,48},{64,56},{72,6... | collective-permute-start | bytes 780296 | tf_op jit(solution)/shard_map/ppermute | solution.py:21
  54.7 0.1 slice_bitcast_fusion.2
  54.9 0.1 maximum_convert_fusion.2
  54.9 0.3 fusion.14
  55.3 0.1 fusion.22
  55.3 6.4 %collective-permute-done.1 = bf16[127,1024]{1,0:T(8,128)(2,1)S(1)} collective-permute-done((bf16[127,1024]{1,0:T(8,128)(2,1)S(1)}, bf16[127,1024]{1,0:T(8,128)(2,1)S(1)}, u32[]{:S(2)}, u32[]{:S(2)}) %collective-permute-start.1) | collective-permute-done | bytes 260128 | tf_op jit(solution)/shard_map/ppermute | solution.py:21
  61.7 0.1 maximum_bitcast_fusion.1
  61.8 14.2 %fusion.6 = f32[1,256,1024]{2,0,1:T(1,128)S(1)} fusion(bf16[1,383,1024]{2,1,0:T(8,128)(2,1)S(1)} %maximum_bitcast_fusion.1, bf16[128,1,1024]{2,0,1:T(8,128)(2,1)S(1)} %bitcast.67), kind=kOutput, calls=%fused_computation.16 | convolution fusion | flops 67108864 | bytes 2095104 | tf_op jit(solution)/shard_map/conv_general_dilated | solution.py:218
  75.9 0.5 multiply_convert_fusion.1
  76.5 0.1 maximum_bitcast_fusion
  76.6 14.2 %fusion.10 = f32[1,256,1024]{2,0,1:T(1,128)S(1)} fusion(bf16[1,383,1024]{2,1,0:T(8,128)(2,1)S(1)} %maximum_bitcast_fusion, bf16[128,1,1024]{2,0,1:T(8,128)(2,1)S(1)} %bitcast.69), kind=kOutput, calls=%fused_computation.22 | convolution fusion | flops 67108864 | bytes 2095104 | tf_op jit(solution)/shard_map/conv_general_dilated | solution.py:218
  90.8 0.3 fusion.18
  91.1 1.2 fusion
  92.4 1.3 pad_maximum_fusion
  93.7 13.9 %fusion.8 = f32[1,128,1024]{2,0,1:T(1,128)S(1)} fusion(bf16[1,383,1024]{2,1,0:T(8,128)(2,1)S(1)} %maximum_bitcast_fusion, bf16[256,1,1024]{2,0,1:T(8,128)(2,1)S(1)} %bitcast.64), kind=kOutput, calls=%fused_computation.20 | convolution fusion | flops 67108864 | bytes 1832960 | tf_op jit(solution)/shard_map/conv_general_dilated | solution.py:218
  107.6 0.1 copy.82
  107.7 0.2 rev.7
  108.1 0.8 slice.161
  108.9 10.9 %collective-permute-start.2 = (bf16[3,2,1024]{2,1,0:T(2,128)(2,1)S(1)}, bf16[3,2,1024]{2,1,0:T(2,128)(2,1)S(1)}, u32[]{:S(2)}, u32[]{:S(2)}) collective-permute-start(bf16[3,2,1024]{2,1,0:T(2,128)(2,1)S(1)} %slice.161), channel_id=1, source_target_pairs={{8,0},{16,8},{24,16},{32,24},{40,32},{48,40},{56,48},{64,56},{72,6... | collective-permute-start | bytes 36872 | tf_op jit(solution)/shard_map/ppermute | solution.py:21
  119.8 0.1 maximum_maximum_fusion.part
  119.9 48.5 %shard_map.67 = (f32[16,8192]{1,0:T(8,128)S(1)}, f32[16,1024]{1,0:T(8,128)S(1)}) custom-call(f32[144,1024]{1,0:T(8,128)S(1)} %maximum_maximum_fusion.part), custom_call_target="tpu_custom_call" | custom-call | tf_op jit(solution)/shard_map/pallas_call | solution.py:187
  168.5 0.6 reshape.21
  169.1 0.0 collective-permute-done.2
  169.1 0.4 maximum_convert_fusion.1
  169.5 2.2 %fusion.4 = bf16[3,256,1024]{2,1,0:T(8,128)(2,1)} fusion(f32[3,258,1024]{2,1,0:T(8,128)S(1)} %maximum_convert_fusion.1, f32[3,1024]{1,0:T(4,128)S(1)} %get-tuple-element.26, f32[3,1024]{1,0:T(4,128)S(1)} %get-tuple-element.27, f32[3,1024]{1,0:T(4,128)S(1)} %bitcast.71), kind=kLoop, calls=%fused_computation.8 | loop fusion | flops 4718592 | bytes 11046912 | tf_op jit(solution)/shard_map/convert_element_type | solution.py:286
  171.6 0.8 copy.87
  (14 shorter events, 0.2 us)
Async XLA Ops:
  0.6 50.5 %copy-start = (bf16[3,256,1024]{2,1,0:T(8,128)(2,1)S(1)}, bf16[3,256,1024]{2,1,0:T(8,128)(2,1)}, u32[]{:S(2)}) copy-start(bf16[3,256,1024]{2,1,0:T(8,128)(2,1)} %param.4) | copy-start | bytes 4718596
  0.6 14.4 %copy-start.2 = (bf16[3,3,1024]{2,1,0:T(4,128)(2,1)S(1)}, bf16[3,3,1024]{2,1,0:T(4,128)(2,1)}, u32[]{:S(2)}) copy-start(bf16[3,3,1024]{2,1,0:T(4,128)(2,1)} %param.7) | copy-start | bytes 55300
  2.4 13.4 %all-to-all-start = ((bf16[16,8,1024]{2,0,1:T(8,128)(2,1)}), bf16[16,8,1024]{2,0,1:T(8,128)(2,1)S(1)}, u32[]{:S(2)}, u32[]{:S(2)}) async-start(bf16[16,8,1024]{2,0,1:T(8,128)(2,1)} %bitcast.59), calls=%async_computation | async-start | bytes 524288 | tf_op jit(solution)/shard_map/all_to_all | solution.py:256
  10.8 40.3 %collective-permute-start = (bf16[260,1024]{1,0:T(8,128)(2,1)S(1)}, bf16[260,1024]{1,0:T(8,128)(2,1)S(1)}, u32[]{:S(2)}, u32[]{:S(2)}) collective-permute-start(bf16[260,1024]{1,0:T(8,128)(2,1)S(1)} %pad_maximum_fusion.1), channel_id=1, source_target_pairs={{0,8},{8,16},{16,24},{24,32},{32,40},{40,48},{48,56},{56,64},{64,7... | collective-permute-start | bytes 1597448 | tf_op jit(solution)/shard_map/ppermute | solution.py:21
  51.6 1.0 copy-start.1
  52.8 8.9 %collective-permute-start.1 = (bf16[127,1024]{1,0:T(8,128)(2,1)S(1)}, bf16[127,1024]{1,0:T(8,128)(2,1)S(1)}, u32[]{:S(2)}, u32[]{:S(2)}) collective-permute-start(bf16[127,1024]{1,0:T(8,128)(2,1)S(1)} %slice.160), channel_id=1, source_target_pairs={{8,0},{16,8},{24,16},{32,24},{40,32},{48,40},{56,48},{64,56},{72,6... | collective-permute-start | bytes 780296 | tf_op jit(solution)/shard_map/ppermute | solution.py:21
  108.9 60.2 %collective-permute-start.2 = (bf16[3,2,1024]{2,1,0:T(2,128)(2,1)S(1)}, bf16[3,2,1024]{2,1,0:T(2,128)(2,1)S(1)}, u32[]{:S(2)}, u32[]{:S(2)}) collective-permute-start(bf16[3,2,1024]{2,1,0:T(2,128)(2,1)S(1)} %slice.161), channel_id=1, source_target_pairs={{8,0},{16,8},{24,16},{32,24},{40,32},{48,40},{56,48},{64,56},{72,6... | collective-permute-start | bytes 36872 | tf_op jit(solution)/shard_map/ppermute | solution.py:21

commit v2 on v1

v2 whole, which is shorter than its diff:
```python
import functools

import jax
import jax.numpy as jnp
import numpy as np
from jax import lax
from jax.experimental import pallas as pl
from jax.experimental.pallas import tpu as pltpu
from jax.sharding import PartitionSpec as P

FILTER_LEN = 128
SHORT_LEN = 3
NX, NYH, NZ = 4, 2, 12
GROUP = 16
LAG = 8
BLOCK = 32
LINK = jnp.float32
MESH = pl.DeviceIdType.MESH
F32, BF16 = jnp.float32, jnp.bfloat16


def basis(length):
    k = np.arange(length // 2, dtype=np.int64)[:, None]
    t = np.arange(length, dtype=np.int64)[None, :]
    angle = np.pi * (((2 * k + 1) * t) % (2 * length)) / length
    return np.concatenate([np.cos(angle), -np.sin(angle)], axis=0)


def split(matrix):
    high = matrix.astype(jnp.bfloat16)
    low = (matrix - high.astype(np.float64)).astype(jnp.bfloat16)
    return high, low


def dot(a, b):
    return jnp.dot(a, b, preferred_element_type=F32)


def fused_kernel(
    nf, inp, go, filt, sw, dh, dl, ih, il,
    ginp, gfilt, gshort,
    pad, wts, kv, mext, gext, taps, ghead, trail, gspec, mspec, stage, zh, zl,
    etail, etail_in, ehead, ehead_in, egrad, egrad_in,
    part, xs, xr, zs, zr, ys, yr, gs, ag,
    s_fil, r_fil, s_edge, r_edge, s_mix, r_mix, s_gl, r_gl,
    sx, rx, sxs, rxs, sz, rz, sy, ry, sg, rg, sh, rh, sa, ra,
):
    seq = lax.axis_index("seq")
    fs = lax.axis_index("fsdp")
    last = NX * NYH * NZ - 1
    z = lax.rem(seq, NZ)
    yh = lax.rem(seq // NZ, NYH)
    x = seq // (NZ * NYH)
    groups = nf + 1
    rows, width = go.shape
    cw = width // NX
    reach = FILTER_LEN
    size = rows + reach
    half = size // 2
    taps_n = nf * GROUP
    assert taps_n == reach
    owner = z < groups
    has_prev = seq > 0
    has_next = seq < last
    scale = 2.0 / size

    def at(ax, ay, az):
        return (ax * NYH + ay) * NZ + az

    def around_x(d):
        return at(lax.rem(x + d, NX), yh, z)

    def around_z(d):
        return at(x, yh, lax.rem(z + d, NZ))

    def around_f(d):
        return lax.rem(fs + d, nf)

    def lanes(c):
        return pl.ds(pl.multiple_of(c * cw, cw), cw)

    across = at(x, 1 - yh, z)

    def remote(src, dst, ssem, rsem, s, f):
        return pltpu.make_async_remote_copy(
            src_ref=src, dst_ref=dst, send_sem=ssem, recv_sem=rsem, device_id=(s, f), device_id_type=MESH
        )

    barrier = pltpu.get_barrier_semaphore()

    def greet(s, f):
        pl.semaphore_signal(barrier, inc=1, device_id=(s, f), device_id_type=MESH)

    pl.when(has_prev)(lambda: greet(seq - 1, fs))
    pl.when(has_next)(lambda: greet(seq + 1, fs))
    for d in range(1, nf):
        greet(seq, around_f(d))
    for d in range(1, NX):
        greet(around_x(d), fs)
    for d in range(1, NZ):
        greet(around_z(d), fs)
    greet(across, fs)
    for f in range(nf):
        pl.when(jnp.logical_or(z != fs, fs != f))(lambda f=f: greet(at(x, yh, fs), f))

    stage[...] = jnp.zeros_like(stage)
    for i in range(3):
        stage[2 * i:2 * i + 2] = inp[i, rows - GROUP:rows].astype(F32)[GROUP - 2:GROUP]
    etail[...] = stage[...].astype(BF16)
    stage[...] = jnp.zeros_like(stage)
    stage[0:2] = inp[0, 0:GROUP].astype(F32)[0:2]
    stage[2:4] = go[0:GROUP].astype(F32)[0:2]
    ehead[...] = stage[...].astype(BF16)
    for i in range(3):
        wts[3 * i:3 * i + 3] = sw[i].astype(F32)

    def tap(i, j, c):
        return wts[3 * i + j:3 * i + j + 1, lanes(c)]

    def short(i, c, lo, n):
        total = tap(i, 0, c) * pad[c, i, LAG + lo:LAG + lo + n]
        for j in range(1, SHORT_LEN):
            total = total + tap(i, j, c) * pad[c, i, LAG + lo - j:LAG + lo - j + n]
        return total

    def mix(c, lo):
        for b in range(lo, lo + reach, BLOCK):
            k = short(1, c, b, BLOCK)
            v = short(2, c, b, BLOCK)
            kv[c, 0, b:b + BLOCK] = k
            kv[c, 1, b:b + BLOCK] = v
            mext[c, reach + b:reach + b + BLOCK] = (k * v).astype(BF16)

    def tail(c, carry):
        for i in range(3):
            pad[c, i, 0:LAG] = jnp.zeros((LAG, cw), F32)
            for b in range(0, rows, BLOCK):
                pad[c, i, LAG + b:LAG + b + BLOCK] = inp[i, b:b + BLOCK, lanes(c)].astype(F32)
        mix(c, rows - reach)
        for b in range(0, reach, BLOCK):
            ghead[c, b:b + BLOCK] = (go[b:b + BLOCK, lanes(c)].astype(F32) * short(0, c, b, BLOCK)).astype(BF16)
        return carry

    lax.fori_loop(0, NX, tail, 0)

    hearers = jnp.where(z < nf, jnp.where(z == fs, NZ - 1, NZ), 0)
    ends = jnp.where(has_prev, 1, 0) + jnp.where(has_next, 1, 0)
    pl.semaphore_wait(barrier, NX - 1 + NZ - 1 + 1 + nf - 1 + hearers + ends)

    def tail_edge():
        return remote(etail, etail_in, s_edge.at[0], r_edge.at[0], seq + 1, fs)

    def head_edge():
        return remote(ehead, ehead_in, s_edge.at[1], r_edge.at[1], seq - 1, fs)

    def grad_edge():
        return remote(egrad, egrad_in, s_edge.at[2], r_edge.at[2], seq - 1, fs)

    def mix_copy(c):
        return remote(mext.at[c, pl.ds(rows, reach)], mext.at[c, pl.ds(0, reach)], s_mix.at[c], r_mix.at[c], seq + 1, fs)

    def long_copy(c):
        return remote(ghead.at[c], gext.at[c, pl.ds(rows, reach)], s_gl.at[c], r_gl.at[c], seq - 1, fs)

    def filt_copy(d):
        f = around_f(d)
        src = filt.at[:, pl.ds(pl.multiple_of(f * width, width), width)]
        dst = taps.at[pl.ds(pl.multiple_of(fs * GROUP, GROUP), GROUP)]
        return remote(src, dst, s_fil.at[d - 1], r_fil.at[d - 1], seq, f)

    @pl.when(has_next)
    def _():
        tail_edge().start()
        for d in range(NX):
            mix_copy(lax.rem(x + 1 + d, NX)).start()

    @pl.when(has_prev)
    def _():
        head_edge().start()
        for d in range(NX):
            long_copy(lax.rem(x + 1 + d, NX)).start()

    for d in range(1, nf):
        filt_copy(d).start()
    taps[pl.ds(pl.multiple_of(fs * GROUP, GROUP), GROUP)] = filt[:, pl.ds(pl.multiple_of(fs * width, width), width)]

    @pl.when(has_prev)
    def _():
        tail_edge().wait_recv()

    @pl.when(jnp.logical_not(has_prev))
    def _():
        etail_in[...] = jnp.zeros_like(etail_in)
        for c in range(NX):
            mext[c, 0:reach] = jnp.zeros((reach, cw), BF16)

    @pl.when(has_next)
    def _():
        head_edge().wait_recv()

    @pl.when(jnp.logical_not(has_next))
    def _():
        ehead_in[...] = jnp.zeros_like(ehead_in)
        egrad_in[...] = jnp.zeros_like(egrad_in)
        for c in range(NX):
            gext[c, rows:size] = jnp.zeros((reach, cw), BF16)

    def rest(c, carry):
        edge = etail_in[:, lanes(c)].astype(F32)
        for i in range(3):
            pad[c, i, LAG - 2:LAG] = edge[2 * i:2 * i + 2]
        mix(c, 0)
        for b in range(0, rows, BLOCK):
            gext[c, b:b + BLOCK] = (go[b:b + BLOCK, lanes(c)].astype(F32) * short(0, c, b, BLOCK)).astype(BF16)
        return carry

    lax.fori_loop(0, NX, rest, 0)

    def forward(signal, lo, n):
        return dot(dh[:, lo:lo + n], signal) + dot(dl[:, lo:lo + n], signal)

    def backward(c, lo, n):
        return scale * (
            dot(ih[lo:lo + n], zh[...]) + (dot(ih[lo:lo + n], zl[...]) + dot(il[lo:lo + n], zh[...]))
        )

    def put(lo, value):
        n = value.shape[0]
        high = value.astype(BF16)
        zh[lo:lo + n] = high
        zl[lo:lo + n] = (value - high.astype(F32)).astype(BF16)

    def product(a, b, c):
        for lo in range(0, half, BLOCK):
            ar, ai = a[c, lo:lo + BLOCK], a[c, half + lo:half + lo + BLOCK]
            br, bi = b[c, lo:lo + BLOCK], b[c, half + lo:half + lo + BLOCK]
            put(lo, ar * br + ai * bi)
            put(half + lo, ai * br - ar * bi)

    def x_copy(d):
        src = (part if LINK == F32 else xs).at[lax.rem(x + 1 + d, NX), pl.ds(0, taps_n)]
        return remote(src, xr.at[d, pl.ds(0, taps_n)], sx.at[d], rx.at[d], around_x(1 + d), fs)

    def xs_copy(d):
        src = (part if LINK == F32 else xs).at[lax.rem(x + 1 + d, NX), pl.ds(taps_n, GROUP)]
        return remote(src, xr.at[d, pl.ds(taps_n, GROUP)], sxs.at[d], rxs.at[d], around_x(1 + d), fs)

    def cross(d, carry):
        c = lax.rem(x + 1 + d, NX)

        @pl.when(has_prev)
        def _():
            mix_copy(c).wait_recv()

        gspec[c] = forward(gext[c, 0:rows], 0, rows)
        mspec[c] = forward(mext[c], 0, size)
        product(gspec, mspec, c)
        terms = -backward(c, rows, reach)
        part[c, 0:taps_n] = terms
        if LINK != F32:
            xs[c, 0:taps_n] = terms.astype(LINK)

        @pl.when(d < NX - 1)
        def _():
            x_copy(d).start()

        return carry

    lax.fori_loop(0, NX, cross, 0)

    for d in range(1, nf):
        filt_copy(d).wait_recv()

    def outputs(d, carry):
        c = lax.rem(x + 1 + d, NX)
        spectrum = forward(taps[:, lanes(c)], 0, reach)

        @pl.when(has_next)
        def _():
            long_copy(c).wait_recv()
            block = gext[c, rows:rows + GROUP].astype(F32)
            edge = ehead_in[:, lanes(c)].astype(F32)
            before = pad[c, 0, LAG + rows - 2:LAG + rows]
            first = tap(0, 0, c) * edge[0:1] + tap(0, 1, c) * before[1:2] + tap(0, 2, c) * before[0:1]
            second = tap(0, 0, c) * edge[1:2] + tap(0, 1, c) * edge[0:1] + tap(0, 2, c) * before[1:2]
            row = lax.broadcasted_iota(jnp.int32, (GROUP, cw), 0)
            block = jnp.where(row == 0, edge[2:3] * first, block)
            block = jnp.where(row == 1, edge[3:4] * second, block)
            gext[c, rows:rows + GROUP] = block.astype(BF16)

        fr, fi = spectrum[:half], spectrum[half:]
        for lo in range(0, half, BLOCK):
            ar, ai = mspec[c, lo:lo + BLOCK], mspec[c, half + lo:half + lo + BLOCK]
            br, bi = fr[lo:lo + BLOCK], fi[lo:lo + BLOCK]
            put(lo, ar * br - ai * bi)
            put(half + lo, ar * bi + ai * br)
        long_out = backward(c, reach, rows)
        trail[c, 0, 0:rows] = (go[:, lanes(c)].astype(F32) * long_out).astype(BF16).astype(F32)
        gspec[c] = gspec[c] + forward(gext[c, rows:size], rows, reach)
        for lo in range(0, half, BLOCK):
            ar, ai = gspec[c, lo:lo + BLOCK], gspec[c, half + lo:half + lo + BLOCK]
            br, bi = fr[lo:lo + BLOCK], fi[lo:lo + BLOCK]
            put(lo, ar * br + ai * bi)
            put(half + lo, ai * br - ar * bi)
        grad_mixed = backward(c, 0, rows)
        trail[c, 1, 0:rows] = (grad_mixed * kv[c, 1]).astype(BF16).astype(F32)
        trail[c, 2, 0:rows] = (grad_mixed * kv[c, 0]).astype(BF16).astype(F32)
        part[c, taps_n:taps_n + GROUP] = jnp.zeros((GROUP, cw), F32)
        for i in range(3):
            sums = [jnp.zeros((8, cw), F32)] * SHORT_LEN
            for b in range(0, rows, BLOCK):
                grads = trail[c, i, b:b + BLOCK]
                for j in range(SHORT_LEN):
                    terms = grads * pad[c, i, LAG + b - j:LAG + b - j + BLOCK]
                    sums[j] = sums[j] + jnp.sum(terms.reshape(BLOCK // 8, 8, cw), axis=0)
            for j in range(SHORT_LEN):
                r = taps_n + 3 * i + j
                part[c, r:r + 1] = jnp.sum(sums[j], axis=0, keepdims=True)
        if LINK != F32:
            xs[c, taps_n:taps_n + GROUP] = part[c, taps_n:taps_n + GROUP].astype(LINK)
        for i in range(3):
            stage[2 * i:2 * i + 2, lanes(c)] = trail[c, i, 0:2]

        @pl.when(d < NX - 1)
        def _():
            xs_copy(d).start()

        return carry

    stage[...] = jnp.zeros_like(stage)
    lax.fori_loop(0, NX, outputs, 0)
    egrad[...] = stage[...].astype(BF16)

    @pl.when(has_prev)
    def _():
        grad_edge().start()

    def z_copy(d):
        return remote(zs.at[lax.rem(z + d, NZ)], zr.at[d - 1], sz.at[d - 1], rz.at[d - 1], around_z(d), fs)

    def y_copy():
        return remote(ys, yr, sy, ry, across, fs)

    def g_copy(d, f):
        return remote(gs, ag.at[x, fs], sg.at[d], rg.at[fs], around_z(d), f)

    def g_landing(f):
        return remote(ag.at[x, f], ag.at[x, f], sg.at[0], rg.at[f], across, fs)

    def h_copy(d):
        return remote(ag.at[x, nf], ag.at[x, nf], sh.at[d - 1], rh, around_z(d), fs)

    def a_copy(d, g):
        return remote(ag.at[x, g], ag.at[x, g], sa.at[d - 1, g], ra.at[d - 1, g], around_x(d), fs)

    def a_landing(d, g):
        back = lax.rem(x + NX - d, NX)
        return remote(ag.at[back, g], ag.at[back, g], sa.at[d - 1, g], ra.at[d - 1, g], around_x(d), fs)

    for d in range(NX - 1):
        x_copy(d).wait_recv()
        xs_copy(d).wait_recv()
    for d in range(1, NZ + 1):
        g = lax.rem(z + d, NZ)

        @pl.when(g < groups)
        def _(d=d, g=g):
            here = pl.ds(pl.multiple_of(g * GROUP, GROUP), GROUP)
            total = part[x, here]
            for e in range(NX - 1):
                total = total + xr[e, here].astype(F32)
            zs[g] = total.astype(zs.dtype)
            if d < NZ:
                z_copy(d).start()

    @pl.when(has_next)
    def _():
        grad_edge().wait_recv()

    def finish(c, carry):
        edge = egrad_in[:, lanes(c)].astype(F32)
        for i in range(3):
            trail[c, i, rows:rows + 2] = edge[2 * i:2 * i + 2]
            for b in range(0, rows, BLOCK):
                total = tap(i, 0, c) * trail[c, i, b:b + BLOCK]
                for j in range(1, SHORT_LEN):
                    total = total + tap(i, j, c) * trail[c, i, b + j:b + j + BLOCK]
                ginp[i, b:b + BLOCK, lanes(c)] = total.astype(BF16)
        return carry

    lax.fori_loop(0, NX, finish, 0)

    @pl.when(owner)
    def _():
        total = zs[z].astype(F32)
        for d in range(1, NZ):
            z_copy(d).wait_recv()
            total = total + zr[d - 1].astype(F32)
        ys[...] = total.astype(ys.dtype)
        y_copy().start()
        y_copy().wait_recv()
        piece = (total + yr[...].astype(F32)).astype(ag.dtype)
        y_copy().wait_send()

        @pl.when(z < nf)
        def _():
            gs[...] = piece

            @pl.when(z == fs)
            def _():
                ag[x, fs] = piece

            for d in range(NZ):
                pl.when(jnp.logical_or(d != 0, z != fs))(lambda d=d: g_copy(d, z).start())

        @pl.when(z == nf)
        def _():
            ag[x, nf] = piece
            for d in range(1, NZ):
                h_copy(d).start()

    for g in range(groups):
        if g < nf:
            pl.when(jnp.logical_or(z != fs, fs != g))(lambda g=g: g_landing(g).wait_recv())
        else:
            pl.when(z != nf)(lambda: h_copy(1).wait_recv())
        for d in range(1, NX):
            a_copy(d, g).start()

    def deliver(c, g):
        if g < nf:
            gfilt[:, pl.ds(pl.multiple_of(g * width + c * cw, cw), cw)] = ag[c, g].astype(F32)
        else:
            for i in range(3):
                gshort[i, :, lanes(c)] = ag[c, g].astype(F32)[3 * i:3 * i + 3]

    for g in range(groups):
        deliver(x, g)
    for g in range(groups):
        for d in range(1, NX):
            a_landing(d, g).wait_recv()
            deliver(lax.rem(x + NX - d, NX), g)

    for d in range(1, nf):
        filt_copy(d).wait_send()
    for d in range(NX - 1):
        x_copy(d).wait_send()
        xs_copy(d).wait_send()

    @pl.when(has_next)
    def _():
        tail_edge().wait_send()
        for c in range(NX):
            mix_copy(c).wait_send()

    @pl.when(has_prev)
    def _():
        head_edge().wait_send()
        grad_edge().wait_send()
        for c in range(NX):
            long_copy(c).wait_send()

    for d in range(1, NZ):
        pl.when(lax.rem(z + d, NZ) < groups)(lambda d=d: z_copy(d).wait_send())

    @pl.when(z < nf)
    def _():
        for d in range(NZ):
            pl.when(jnp.logical_or(d != 0, z != fs))(lambda d=d: g_copy(d, z).wait_send())

    @pl.when(z == nf)
    def _():
        for d in range(1, NZ):
            h_copy(d).wait_send()

    for g in range(groups):
        for d in range(1, NX):
            a_copy(d, g).wait_send()


def local(inputs, grad_out, filters, short_weights):
    rows, width = grad_out.shape
    nf = lax.axis_size("fsdp")
    cw = width // NX
    size = rows + FILTER_LEN
    matrix = basis(size)
    dh, dl = split(matrix)
    ih, il = (np.ascontiguousarray(m.T) for m in (dh, dl))
    part_rows = (nf + 1) * GROUP
    dma = pltpu.SemaphoreType.DMA
    vm = pl.BlockSpec(memory_space=pltpu.VMEM)
    return pl.pallas_call(
        functools.partial(fused_kernel, nf),
        out_shape=(
            jax.ShapeDtypeStruct(inputs.shape, BF16),
            jax.ShapeDtypeStruct((GROUP, nf * width), F32),
            jax.ShapeDtypeStruct((3, SHORT_LEN, width), F32),
        ),
        in_specs=[vm] * 8,
        out_specs=(vm,) * 3,
        scratch_shapes=[
            pltpu.VMEM((NX, 3, LAG + rows, cw), F32),
            pltpu.VMEM((GROUP, width), F32),
            pltpu.VMEM((NX, 2, rows, cw), F32),
            pltpu.VMEM((NX, size, cw), BF16),
            pltpu.VMEM((NX, size, cw), BF16),
            pltpu.VMEM((FILTER_LEN, width), BF16),
            pltpu.VMEM((NX, FILTER_LEN, cw), BF16),
            pltpu.VMEM((NX, 3, rows + LAG, cw), F32),
            pltpu.VMEM((NX, size, cw), F32),
            pltpu.VMEM((NX, size, cw), F32),
            pltpu.VMEM((GROUP, width), F32),
            pltpu.VMEM((size, cw), BF16),
            pltpu.VMEM((size, cw), BF16),
            *[pltpu.VMEM((GROUP, width), BF16)] * 6,
            pltpu.VMEM((NX, part_rows, cw), F32),
            pltpu.VMEM((NX, part_rows, cw), LINK),
            pltpu.VMEM((NX - 1, part_rows, cw), LINK),
            pltpu.VMEM((NZ, GROUP, cw), LINK),
            pltpu.VMEM((NZ - 1, GROUP, cw), LINK),
            pltpu.VMEM((GROUP, cw), LINK),
            pltpu.VMEM((GROUP, cw), LINK),
            pltpu.VMEM((GROUP, cw), LINK),
            pltpu.VMEM((NX, nf + 1, GROUP, cw), LINK),
            dma((nf - 1,)), dma((nf - 1,)),
            dma((3,)), dma((3,)),
            dma((NX,)), dma((NX,)),
            dma((NX,)), dma((NX,)),
            dma((NX - 1,)), dma((NX - 1,)),
            dma((NX - 1,)), dma((NX - 1,)),
            dma((NZ - 1,)), dma((NZ - 1,)),
            dma, dma,
            dma((NZ,)), dma((nf,)),
            dma((NZ - 1,)), dma,
            dma((NX - 1, nf + 1)), dma((NX - 1, nf + 1)),
        ],
        compiler_params=pltpu.CompilerParams(
            collective_id=0, has_side_effects=True, vmem_limit_bytes=56 * 1024 * 1024
        ),
    )(inputs, grad_out, filters, short_weights, dh, dl, ih, il)


def solution(mesh):
    placed = (P(None, "seq", "fsdp"), P("seq", "fsdp"), P("fsdp", None), P(None, None, "fsdp"))
    return jax.shard_map(
        local,
        mesh=mesh,
        in_specs=placed,
        out_specs=(P(None, "seq", "fsdp"), P("fsdp", None), P(None, None, "fsdp")),
        check_vma=False,
    )
```

time: 173 us -> 86.1 us (0.50)
  the two profiles are of different devices: /device:TPU:56 before, /device:TPU:24 now
where the time goes in v2:
time: 86.1 us; the launch traced here: 85.9 us
  Pallas kernels  81.1 us (94%)
  local copies, waits for them, and re-layouts  4.15 us (5%)
    pallas_call x1, Pallas kernels, local(): pl.pallas_call(functools.partial(fused_kernel, nf), out_shape=(jax.ShapeD...  81.1 us
    unnamed x7, local copies, waits for them, and re-layouts  4.15 us

profile of v2, /device:TPU:24, one launch (start us, length us, event | category | flops | bytes accessed | tf_op | source)
XLA Modules:
  0.0 85.9 jit_solution(15620062950995489884)
XLA Ops:
  0.6 81.1 %shard_map.103 = (bf16[3,256,1024]{2,1,0:T(8,128)(2,1)}, f32[16,8192]{1,0:T(8,128)}, f32[3,3,1024]{2,1,0:T(4,128)}) custom-call(bf16[3,256,1024]{2,1,0:T(8,128)(2,1)} %inp.1, bf16[256,1024]{1,0:T(8,128)(2,1)} %go.1, bf16[16,8192]{1,0:T(8,128)(2,1)} %filt.1, bf16[3,3,1024]{2,1,0:T(4,128)(2,1)} %sw.1, bf16[384,384]{1,0:T(8,128)(2,1)} %constant.8.clone.dh, ...), custom_call_target="tpu_custom_call" | custom-call | tf_op jit(solution)/shard_map/pallas_call | solution.py:492
  81.7 0.0 copy-start
  81.7 0.0 copy-start.1
  81.8 2.7 %copy.14 = bf16[3,256,1024]{2,1,0:T(8,128)(2,1)} copy(bf16[3,256,1024]{2,1,0:T(8,128)(2,1)} %get-tuple-element.6) | data formatting | bytes 3145728
  84.5 0.0 copy-done
  84.5 0.8 copy.15
  85.3 0.0 copy-done.1
  85.3 0.6 copy.16
Async XLA Ops:
  81.7 2.7 %copy-start = (f32[16,8192]{1,0:T(8,128)S(1)}, f32[16,8192]{1,0:T(8,128)}, u32[]{:S(2)}) copy-start(f32[16,8192]{1,0:T(8,128)} %get-tuple-element.7) | copy-start | bytes 1572868
  81.7 3.5 %copy-start.1 = (f32[3,3,1024]{2,1,0:T(4,128)S(1)}, f32[3,3,1024]{2,1,0:T(4,128)}, u32[]{:S(2)}) copy-start(f32[3,3,1024]{2,1,0:T(4,128)} %get-tuple-element.8) | copy-start | bytes 110596

commit v3 on v2

--- a/solution.py
+++ b/solution.py
@@ -14,7 +14,7 @@
 GROUP = 16
 LAG = 8
 BLOCK = 32
-LINK = jnp.float32
+LINK = jnp.bfloat16
 MESH = pl.DeviceIdType.MESH
 F32, BF16 = jnp.float32, jnp.bfloat16
 
@@ -37,8 +37,9 @@
 
 
 def fused_kernel(
-    nf, inp, go, filt, sw, dh, dl, ih, il,
-    ginp, gfilt, gshort,
+    nf, inp_in, go_in, filt_in, sw_in, fwd_in, bwd_in,
+    ginp_out, gfilt, gshort,
+    inp, go, filt, sw, fwd, bwd, ginp, s_in, s_out,
     pad, wts, kv, mext, gext, taps, ghead, trail, gspec, mspec, stage, zh, zl,
     etail, etail_in, ehead, ehead_in, egrad, egrad_in,
     part, xs, xr, zs, zr, ys, yr, gs, ag,
@@ -62,7 +63,16 @@
     owner = z < groups
     has_prev = seq > 0
     has_next = seq < last
-    scale = 2.0 / size
+    far_z = sorted(range(1, NZ), key=lambda d: abs(2 * d - NZ))
+    far_x = sorted(range(1, NX), key=lambda d: abs(2 * d - NX))
+    loads = [
+        pltpu.make_async_copy(a, b, s_in.at[n])
+        for n, (a, b) in enumerate(
+            ((inp_in, inp), (go_in, go), (sw_in, sw), (filt_in, filt), (fwd_in, fwd), (bwd_in, bwd))
+        )
+    ]
+    for load in loads:
+        load.start()
 
     def at(ax, ay, az):
         return (ax * NYH + ay) * NZ + az
@@ -103,6 +113,9 @@
     for f in range(nf):
         pl.when(jnp.logical_or(z != fs, fs != f))(lambda f=f: greet(at(x, yh, fs), f))
 
+    for load in loads[:3]:
+        load.wait()
+
     stage[...] = jnp.zeros_like(stage)
     for i in range(3):
         stage[2 * i:2 * i + 2] = inp[i, rows - GROUP:rows].astype(F32)[GROUP - 2:GROUP]
@@ -146,6 +159,7 @@
     hearers = jnp.where(z < nf, jnp.where(z == fs, NZ - 1, NZ), 0)
     ends = jnp.where(has_prev, 1, 0) + jnp.where(has_next, 1, 0)
     pl.semaphore_wait(barrier, NX - 1 + NZ - 1 + 1 + nf - 1 + hearers + ends)
+    loads[3].wait()
 
     def tail_edge():
         return remote(etail, etail_in, s_edge.at[0], r_edge.at[0], seq + 1, fs)
@@ -168,17 +182,12 @@
         dst = taps.at[pl.ds(pl.multiple_of(fs * GROUP, GROUP), GROUP)]
         return remote(src, dst, s_fil.at[d - 1], r_fil.at[d - 1], seq, f)
 
-    @pl.when(has_next)
-    def _():
-        tail_edge().start()
-        for d in range(NX):
-            mix_copy(lax.rem(x + 1 + d, NX)).start()
-
-    @pl.when(has_prev)
-    def _():
-        head_edge().start()
-        for d in range(NX):
-            long_copy(lax.rem(x + 1 + d, NX)).start()
+    pl.when(has_next)(lambda: tail_edge().start())
+    pl.when(has_prev)(lambda: head_edge().start())
+    for d in range(NX):
+        pl.when(has_next)(lambda d=d: mix_copy(lax.rem(x + 1 + d, NX)).start())
+    for d in range(NX):
+        pl.when(has_prev)(lambda d=d: long_copy(lax.rem(x + 1 + d, NX)).start())
 
     for d in range(1, nf):
         filt_copy(d).start()
@@ -216,13 +225,16 @@
 
     lax.fori_loop(0, NX, rest, 0)
 
+    for load in loads[4:]:
+        load.wait()
+
     def forward(signal, lo, n):
-        return dot(dh[:, lo:lo + n], signal) + dot(dl[:, lo:lo + n], signal)
-
-    def backward(c, lo, n):
-        return scale * (
-            dot(ih[lo:lo + n], zh[...]) + (dot(ih[lo:lo + n], zl[...]) + dot(il[lo:lo + n], zh[...]))
-        )
+        both = dot(fwd[:, lo:lo + n], signal)
+        return both[:size] + both[size:]
+
+    def backward(row, n):
+        both = dot(bwd[row:row + 2 * n], zh[...])
+        return both[:n] + (both[n:] + dot(bwd[row:row + n], zl[...]))
 
     def put(lo, value):
         n = value.shape[0]
@@ -245,6 +257,13 @@
         src = (part if LINK == F32 else xs).at[lax.rem(x + 1 + d, NX), pl.ds(taps_n, GROUP)]
         return remote(src, xr.at[d, pl.ds(taps_n, GROUP)], sxs.at[d], rxs.at[d], around_x(1 + d), fs)
 
+    def spectra(c, carry):
+        gspec[c] = forward(gext[c, 0:rows], 0, rows)
+        mspec[c] = forward(mext[c, reach:size], reach, rows)
+        return carry
+
+    lax.fori_loop(0, NX, spectra, 0)
+
     def cross(d, carry):
         c = lax.rem(x + 1 + d, NX)
 
@@ -252,10 +271,9 @@
         def _():
             mix_copy(c).wait_recv()
 
-        gspec[c] = forward(gext[c, 0:rows], 0, rows)
-        mspec[c] = forward(mext[c], 0, size)
+        mspec[c] = mspec[c] + forward(mext[c, 0:reach], 0, reach)
         product(gspec, mspec, c)
-        terms = -backward(c, rows, reach)
+        terms = backward(0, reach)
         part[c, 0:taps_n] = terms
         if LINK != F32:
             xs[c, 0:taps_n] = terms.astype(LINK)
@@ -294,7 +312,7 @@
             br, bi = fr[lo:lo + BLOCK], fi[lo:lo + BLOCK]
             put(lo, ar * br - ai * bi)
             put(half + lo, ar * bi + ai * br)
-        long_out = backward(c, reach, rows)
+        long_out = backward(2 * reach, rows)
         trail[c, 0, 0:rows] = (go[:, lanes(c)].astype(F32) * long_out).astype(BF16).astype(F32)
         gspec[c] = gspec[c] + forward(gext[c, rows:size], rows, reach)
         for lo in range(0, half, BLOCK):
@@ -302,7 +320,7 @@
             br, bi = fr[lo:lo + BLOCK], fi[lo:lo + BLOCK]
             put(lo, ar * br + ai * bi)
             put(half + lo, ai * br - ar * bi)
-        grad_mixed = backward(c, 0, rows)
+        grad_mixed = backward(2 * reach + 2 * rows, rows)
         trail[c, 1, 0:rows] = (grad_mixed * kv[c, 1]).astype(BF16).astype(F32)
         trail[c, 2, 0:rows] = (grad_mixed * kv[c, 0]).astype(BF16).astype(F32)
         part[c, taps_n:taps_n + GROUP] = jnp.zeros((GROUP, cw), F32)
@@ -360,22 +378,28 @@
     for d in range(NX - 1):
         x_copy(d).wait_recv()
         xs_copy(d).wait_recv()
-    for d in range(1, NZ + 1):
+
+    def x_total(g):
+        here = pl.ds(pl.multiple_of(g * GROUP, GROUP), GROUP)
+        total = part[x, here]
+        for e in range(NX - 1):
+            total = total + xr[e, here].astype(F32)
+        return total
+
+    for d in far_z:
         g = lax.rem(z + d, NZ)
 
         @pl.when(g < groups)
         def _(d=d, g=g):
-            here = pl.ds(pl.multiple_of(g * GROUP, GROUP), GROUP)
-            total = part[x, here]
-            for e in range(NX - 1):
-                total = total + xr[e, here].astype(F32)
-            zs[g] = total.astype(zs.dtype)
-            if d < NZ:
-                z_copy(d).start()
+            zs[g] = x_total(g).astype(zs.dtype)
+            z_copy(d).start()
 
     @pl.when(has_next)
     def _():
         grad_edge().wait_recv()
+
+    def out_copy(c):
+        return pltpu.make_async_copy(ginp.at[:, :, lanes(c)], ginp_out.at[:, :, lanes(c)], s_out.at[c])
 
     def finish(c, carry):
         edge = egrad_in[:, lanes(c)].astype(F32)
@@ -386,20 +410,21 @@
                 for j in range(1, SHORT_LEN):
                     total = total + tap(i, j, c) * trail[c, i, b + j:b + j + BLOCK]
                 ginp[i, b:b + BLOCK, lanes(c)] = total.astype(BF16)
+        out_copy(c).start()
         return carry
 
     lax.fori_loop(0, NX, finish, 0)
 
     @pl.when(owner)
     def _():
-        total = zs[z].astype(F32)
+        total = x_total(z)
         for d in range(1, NZ):
             z_copy(d).wait_recv()
             total = total + zr[d - 1].astype(F32)
-        ys[...] = total.astype(ys.dtype)
+        ys[...] = total
         y_copy().start()
         y_copy().wait_recv()
-        piece = (total + yr[...].astype(F32)).astype(ag.dtype)
+        piece = (total + yr[...]).astype(ag.dtype)
         y_copy().wait_send()
 
         @pl.when(z < nf)
@@ -410,13 +435,13 @@
             def _():
                 ag[x, fs] = piece
 
-            for d in range(NZ):
+            for d in far_z + [0]:
                 pl.when(jnp.logical_or(d != 0, z != fs))(lambda d=d: g_copy(d, z).start())
 
         @pl.when(z == nf)
         def _():
             ag[x, nf] = piece
-            for d in range(1, NZ):
+            for d in far_z:
                 h_copy(d).start()
 
     for g in range(groups):
@@ -424,7 +449,7 @@
             pl.when(jnp.logical_or(z != fs, fs != g))(lambda g=g: g_landing(g).wait_recv())
         else:
             pl.when(z != nf)(lambda: h_copy(1).wait_recv())
-        for d in range(1, NX):
+        for d in far_x:
             a_copy(d, g).start()
 
     def deliver(c, g):
@@ -450,15 +475,17 @@
     @pl.when(has_next)
     def _():
         tail_edge().wait_send()
-        for c in range(NX):
-            mix_copy(c).wait_send()
 
     @pl.when(has_prev)
     def _():
         head_edge().wait_send()
         grad_edge().wait_send()
-        for c in range(NX):
-            long_copy(c).wait_send()
+
+    for c in range(NX):
+        pl.when(has_next)(lambda c=c: mix_copy(c).wait_send())
+        pl.when(has_prev)(lambda c=c: long_copy(c).wait_send())
+    for c in range(NX):
+        out_copy(c).wait()
 
     for d in range(1, NZ):
         pl.when(lax.rem(z + d, NZ) < groups)(lambda d=d: z_copy(d).wait_send())
@@ -476,6 +503,38 @@
     for g in range(groups):
         for d in range(1, NX):
             a_copy(d, g).wait_send()
+
+
+def copy_kernel(n, *refs):
+    held, sems_in, sems_out = refs[2 * n:3 * n], refs[3 * n], refs[3 * n + 1]
+    parts = []
+    for src, dst, via in zip(refs[:n], refs[n:2 * n], held):
+        if src.dtype == BF16:
+            parts += [(src.at[i], via.at[i], dst.at[i]) for i in range(src.shape[0])]
+        else:
+            parts.append((src, via, dst))
+    into = [pltpu.make_async_copy(a, b, sems_in.at[k]) for k, (a, b, _) in enumerate(parts)]
+    out = [pltpu.make_async_copy(b, c, sems_out.at[k]) for k, (_, b, c) in enumerate(parts)]
+    for copy in into:
+        copy.start()
+    for a, b in zip(into, out):
+        a.wait()
+        b.start()
+    for copy in out:
+        copy.wait()
+
+
+def placed(results):
+    anywhere = pl.BlockSpec(memory_space=pl.ANY)
+    n = len(results)
+    return pl.pallas_call(
+        functools.partial(copy_kernel, n),
+        out_shape=tuple(jax.ShapeDtypeStruct(r.shape, r.dtype) for r in results),
+        in_specs=[anywhere] * n,
+        out_specs=(anywhere,) * n,
+        scratch_shapes=[pltpu.VMEM(r.shape, r.dtype) for r in results] + [pltpu.SemaphoreType.DMA((5,))] * 2,
+        compiler_params=pltpu.CompilerParams(vmem_limit_bytes=60 * 1024 * 1024),
+    )(*results)
 
 
 def local(inputs, grad_out, filters, short_weights):
@@ -484,21 +543,32 @@
     cw = width // NX
     size = rows + FILTER_LEN
     matrix = basis(size)
-    dh, dl = split(matrix)
-    ih, il = (np.ascontiguousarray(m.T) for m in (dh, dl))
+    fwd = np.concatenate(split(matrix), axis=0)
+    inverse = matrix.T * (2.0 / size)
+    pieces = (-inverse[rows:], inverse[FILTER_LEN:], inverse[:rows])
+    bwd = np.concatenate([half for piece in pieces for half in split(piece)], axis=0)
     part_rows = (nf + 1) * GROUP
     dma = pltpu.SemaphoreType.DMA
     vm = pl.BlockSpec(memory_space=pltpu.VMEM)
-    return pl.pallas_call(
+    anywhere = pl.BlockSpec(memory_space=pl.ANY)
+    results = pl.pallas_call(
         functools.partial(fused_kernel, nf),
         out_shape=(
             jax.ShapeDtypeStruct(inputs.shape, BF16),
             jax.ShapeDtypeStruct((GROUP, nf * width), F32),
             jax.ShapeDtypeStruct((3, SHORT_LEN, width), F32),
         ),
-        in_specs=[vm] * 8,
-        out_specs=(vm,) * 3,
+        in_specs=[anywhere] * 6,
+        out_specs=(anywhere, vm, vm),
         scratch_shapes=[
+            pltpu.VMEM(inputs.shape, BF16),
+            pltpu.VMEM(grad_out.shape, BF16),
+            pltpu.VMEM(filters.shape, BF16),
+            pltpu.VMEM(short_weights.shape, BF16),
+            pltpu.VMEM(fwd.shape, BF16),
+            pltpu.VMEM(bwd.shape, BF16),
+            pltpu.VMEM(inputs.shape, BF16),
+            dma((6,)), dma((NX,)),
             pltpu.VMEM((NX, 3, LAG + rows, cw), F32),
             pltpu.VMEM((GROUP, width), F32),
             pltpu.VMEM((NX, 2, rows, cw), F32),
@@ -518,8 +588,8 @@
             pltpu.VMEM((NX - 1, part_rows, cw), LINK),
             pltpu.VMEM((NZ, GROUP, cw), LINK),
             pltpu.VMEM((NZ - 1, GROUP, cw), LINK),
-            pltpu.VMEM((GROUP, cw), LINK),
-            pltpu.VMEM((GROUP, cw), LINK),
+            pltpu.VMEM((GROUP, cw), F32),
+            pltpu.VMEM((GROUP, cw), F32),
             pltpu.VMEM((GROUP, cw), LINK),
             pltpu.VMEM((NX, nf + 1, GROUP, cw), LINK),
             dma((nf - 1,)), dma((nf - 1,)),
@@ -537,7 +607,8 @@
         compiler_params=pltpu.CompilerParams(
             collective_id=0, has_side_effects=True, vmem_limit_bytes=56 * 1024 * 1024
         ),
-    )(inputs, grad_out, filters, short_weights, dh, dl, ih, il)
+    )(inputs, grad_out, filters, short_weights, fwd, bwd)
+    return placed(results)
 
 
 def solution(mesh):

time: 86.1 us -> 74.3 us (0.86)
  Pallas kernels: 81.1 us -> 73.5 us
  local copies, waits for them, and re-layouts: 4.15 us -> 0 us
    pallas_call x1, Pallas kernels: 81.1 us -> 71.1 us  [local(): pl.pallas_call(functools.partial(fused_kernel, nf), out_shape=(jax.ShapeD...]
    unnamed x7 -> x0, local copies, waits for them, and re-layouts: 4.15 us -> none
    pallas_call x0 -> x1, Pallas kernels: none -> 2.44 us  [placed(): pl.pallas_call(functools.partial(copy_kernel, n), out_shape=tuple((jax.Sh...]
where the time goes in v3:
time: 74.3 us; the launch traced here: 74.2 us
  Pallas kernels  73.5 us (99%)
    pallas_call x1, Pallas kernels, local(): pl.pallas_call(functools.partial(fused_kernel, nf), out_shape=(jax.ShapeD...  71.1 us
    pallas_call x1, Pallas kernels, placed(): pl.pallas_call(functools.partial(copy_kernel, n), out_shape=tuple((jax.Sh...  2.44 us

profile of v3, /device:TPU:24, one launch (start us, length us, event | category | flops | bytes accessed | tf_op | source)
XLA Modules:
  0.0 74.2 jit_solution(8625779472505733580)
XLA Ops:
  0.6 71.1 %shard_map.85 = (bf16[3,256,1024]{2,1,0:T(8,128)(2,1)}, f32[16,8192]{1,0:T(8,128)}, f32[3,3,1024]{2,1,0:T(4,128)}) custom-call(bf16[3,256,1024]{2,1,0:T(8,128)(2,1)} %inp_in.1, bf16[256,1024]{1,0:T(8,128)(2,1)} %go_in.1, bf16[16,8192]{1,0:T(8,128)(2,1)} %filt_in.1, bf16[3,3,1024]{2,1,0:T(4,128)(2,1)} %sw_in.1, bf16[768,384]{1,0:T(8,128)(2,1)} %constant.4.clone.fwd_in, ...), custom_call_target="tpu_custom_call" | custom-call | tf_op jit(solution)/shard_map/pallas_call | solution.py:554
  71.7 2.4 %shard_map.86 = (bf16[3,256,1024]{2,1,0:T(8,128)(2,1)}, f32[16,8192]{1,0:T(8,128)}, f32[3,3,1024]{2,1,0:T(4,128)}) custom-call(bf16[3,256,1024]{2,1,0:T(8,128)(2,1)} %get-tuple-element.6.refs_0_, f32[16,8192]{1,0:T(8,128)} %get-tuple-element.7.refs_1_, f32[3,3,1024]{2,1,0:T(4,128)} %get-tuple-element.8.refs_2_), custom_call_target="tpu_custom_call" | custom-call | tf_op jit(solution)/shard_map/pallas_call | solution.py:530

commit v4 on v3

--- a/solution.py
+++ b/solution.py
@@ -38,8 +38,8 @@
 
 def fused_kernel(
     nf, inp_in, go_in, filt_in, sw_in, fwd_in, bwd_in,
-    ginp_out, gfilt, gshort,
-    inp, go, filt, sw, fwd, bwd, ginp, s_in, s_out,
+    ginp, gfilt, gshort,
+    inp, go, filt, sw, fwd, bwd, s_in,
     pad, wts, kv, mext, gext, taps, ghead, trail, gspec, mspec, stage, zh, zl,
     etail, etail_in, ehead, ehead_in, egrad, egrad_in,
     part, xs, xr, zs, zr, ys, yr, gs, ag,
@@ -398,9 +398,6 @@
     def _():
         grad_edge().wait_recv()
 
-    def out_copy(c):
-        return pltpu.make_async_copy(ginp.at[:, :, lanes(c)], ginp_out.at[:, :, lanes(c)], s_out.at[c])
-
     def finish(c, carry):
         edge = egrad_in[:, lanes(c)].astype(F32)
         for i in range(3):
@@ -410,7 +407,6 @@
                 for j in range(1, SHORT_LEN):
                     total = total + tap(i, j, c) * trail[c, i, b + j:b + j + BLOCK]
                 ginp[i, b:b + BLOCK, lanes(c)] = total.astype(BF16)
-        out_copy(c).start()
         return carry
 
     lax.fori_loop(0, NX, finish, 0)
@@ -484,8 +480,6 @@
     for c in range(NX):
         pl.when(has_next)(lambda c=c: mix_copy(c).wait_send())
         pl.when(has_prev)(lambda c=c: long_copy(c).wait_send())
-    for c in range(NX):
-        out_copy(c).wait()
 
     for d in range(1, NZ):
         pl.when(lax.rem(z + d, NZ) < groups)(lambda d=d: z_copy(d).wait_send())
@@ -503,38 +497,6 @@
     for g in range(groups):
         for d in range(1, NX):
             a_copy(d, g).wait_send()
-
-
-def copy_kernel(n, *refs):
-    held, sems_in, sems_out = refs[2 * n:3 * n], refs[3 * n], refs[3 * n + 1]
-    parts = []
-    for src, dst, via in zip(refs[:n], refs[n:2 * n], held):
-        if src.dtype == BF16:
-            parts += [(src.at[i], via.at[i], dst.at[i]) for i in range(src.shape[0])]
-        else:
-            parts.append((src, via, dst))
-    into = [pltpu.make_async_copy(a, b, sems_in.at[k]) for k, (a, b, _) in enumerate(parts)]
-    out = [pltpu.make_async_copy(b, c, sems_out.at[k]) for k, (_, b, c) in enumerate(parts)]
-    for copy in into:
-        copy.start()
-    for a, b in zip(into, out):
-        a.wait()
-        b.start()
-    for copy in out:
-        copy.wait()
-
-
-def placed(results):
-    anywhere = pl.BlockSpec(memory_space=pl.ANY)
-    n = len(results)
-    return pl.pallas_call(
-        functools.partial(copy_kernel, n),
-        out_shape=tuple(jax.ShapeDtypeStruct(r.shape, r.dtype) for r in results),
-        in_specs=[anywhere] * n,
-        out_specs=(anywhere,) * n,
-        scratch_shapes=[pltpu.VMEM(r.shape, r.dtype) for r in results] + [pltpu.SemaphoreType.DMA((5,))] * 2,
-        compiler_params=pltpu.CompilerParams(vmem_limit_bytes=60 * 1024 * 1024),
-    )(*results)
 
 
 def local(inputs, grad_out, filters, short_weights):
@@ -554,12 +516,12 @@
     results = pl.pallas_call(
         functools.partial(fused_kernel, nf),
         out_shape=(
-            jax.ShapeDtypeStruct(inputs.shape, BF16),
-            jax.ShapeDtypeStruct((GROUP, nf * width), F32),
-            jax.ShapeDtypeStruct((3, SHORT_LEN, width), F32),
+            pltpu.VMEM(inputs.shape, BF16),
+            pltpu.VMEM((GROUP, nf * width), F32),
+            pltpu.VMEM((3, SHORT_LEN, width), F32),
         ),
         in_specs=[anywhere] * 6,
-        out_specs=(anywhere, vm, vm),
+        out_specs=(vm, vm, vm),
         scratch_shapes=[
             pltpu.VMEM(inputs.shape, BF16),
             pltpu.VMEM(grad_out.shape, BF16),
@@ -567,8 +529,7 @@
             pltpu.VMEM(short_weights.shape, BF16),
             pltpu.VMEM(fwd.shape, BF16),
             pltpu.VMEM(bwd.shape, BF16),
-            pltpu.VMEM(inputs.shape, BF16),
-            dma((6,)), dma((NX,)),
+            dma((6,)),
             pltpu.VMEM((NX, 3, LAG + rows, cw), F32),
             pltpu.VMEM((GROUP, width), F32),
             pltpu.VMEM((NX, 2, rows, cw), F32),
@@ -608,7 +569,7 @@
             collective_id=0, has_side_effects=True, vmem_limit_bytes=56 * 1024 * 1024
         ),
     )(inputs, grad_out, filters, short_weights, fwd, bwd)
-    return placed(results)
+    return tuple(results)
 
 
 def solution(mesh):

time: 74.3 us -> 73.6 us (level)
  Pallas kernels: 73.5 us -> 70.2 us
  local copies, waits for them, and re-layouts: 0 us -> 2.56 us
    pallas_call x2 -> x1, Pallas kernels: 73.5 us -> 70.2 us  [local(): pl.pallas_call(functools.partial(fused_kernel, nf), out_shape=(pltpu.VMEM...]
    unnamed x0 -> x3, local copies, waits for them, and re-layouts: none -> 2.56 us
where the time goes in v4:
time: 73.6 us; the launch traced here: 73.4 us
  Pallas kernels  70.2 us (95%)
  local copies, waits for them, and re-layouts  2.56 us (3%)
    pallas_call x1, Pallas kernels, local(): pl.pallas_call(functools.partial(fused_kernel, nf), out_shape=(pltpu.VMEM...  70.2 us
    unnamed x3, local copies, waits for them, and re-layouts  2.56 us

profile of v4, /device:TPU:24, one launch (start us, length us, event | category | flops | bytes accessed | tf_op | source)
XLA Modules:
  0.0 73.4 jit_solution(14032032324512411654)
XLA Ops:
  0.6 70.2 %shard_map.85 = (bf16[3,256,1024]{2,1,0:T(8,128)(2,1)S(1)}, f32[16,8192]{1,0:T(8,128)S(1)}, f32[3,3,1024]{2,1,0:T(4,128)S(1)}) custom-call(bf16[3,256,1024]{2,1,0:T(8,128)(2,1)} %inp_in.1, bf16[256,1024]{1,0:T(8,128)(2,1)} %go_in.1, bf16[16,8192]{1,0:T(8,128)(2,1)} %filt_in.1, bf16[3,3,1024]{2,1,0:T(4,128)(2,1)} %sw_in.1, ...), custom_call_target="tpu_custom_call" | custom-call | tf_op jit(solution)/shard_map/pallas_call | solution.py:516
  70.9 1.1 %copy.12 = bf16[3,256,1024]{2,1,0:T(8,128)(2,1)} copy(bf16[3,256,1024]{2,1,0:T(8,128)(2,1)S(1)} %get-tuple-element.3) | data formatting | bytes 3145728
  72.0 0.6 copy.14
  72.7 0.8 %copy.13 = f32[16,8192]{1,0:T(8,128)} copy(f32[16,8192]{1,0:T(8,128)S(1)} %get-tuple-element.4) | data formatting | bytes 1048576
